TPU v7x, 512 devices: a whole 4x4x16 slice. The times are simulated.
512 devices in a mesh: user: 16 (over y, x), item: 32 (over z, core).
Axes of the slice: x: 4, y: 4, z: 16, core: 2. Of those that a mesh axis runs over, the one named last changes fastest.
Arguments:
- panel_users: bfloat16 [8192, 256], P(('user', 'item'))
- block_values: bfloat16 [8192, 224, 128], P('user', 'item')
- block_list: int32 [16, 224], P('user', 'item'), may hold values from 0 to 7, as said below
- block_count: int32 [16, 32], P('user', 'item'), may hold values from 1 to 7, as said below
Outputs:
- factor_diag: float32 [256, 256], replicated
- factor_below: float32 [32768, 256], P('item')
Inputs may be any that keep to these rules, and one draw needn't show every extreme that they name: `block_list`: within one user shard and item index the first block_count slots name distinct row blocks. `block_count`: some device uses all slots.
All inputs are finite; a program needn't handle non-finite values.
Results may differ from a plain program's by a relative error of at most 0.0003.
Values may be sent and summed in bfloat16 or wider, within the bound.
A program may use at most 64 MiB of HBM per device.

v0:
```python
import jax
import jax.numpy as jnp
from jax import lax
from jax.sharding import PartitionSpec as P

BLOCK = 128
PANEL = 256
BLK_DEV = 8


def solve_rows(factor_diag, rows):
    return lax.linalg.triangular_solve(
        factor_diag, rows, left_side=False, lower=True, transpose_a=True
    )


def on_device(panel_users, block_values, block_list, block_count):
    gathered = lax.all_gather(panel_users, "item", axis=0, tiled=True)
    diag_part = jnp.dot(gathered.T, gathered, preferred_element_type=jnp.float32)
    product = jnp.einsum("ukc,up->kcp", block_values, gathered, preferred_element_type=jnp.float32)
    slot_count = block_values.shape[1]
    blocks_here = jnp.arange(BLK_DEV, dtype=jnp.int32)
    slots_here = jnp.arange(slot_count, dtype=jnp.int32)
    identity = 0.5 * jnp.eye(PANEL, dtype=jnp.float32)
    chosen = (block_list[0][:, None] == blocks_here[None, :]) & (
        slots_here[:, None] < block_count[0, 0]
    )
    placed = jnp.einsum(
        "kb,kcp->bcp", chosen.astype(jnp.float32), product, precision=lax.Precision.HIGHEST
    )
    below_part = placed.reshape(BLK_DEV * BLOCK, PANEL)
    diag_total, below_total = lax.psum((diag_part, below_part), "user")
    factor_diag = jnp.linalg.cholesky(diag_total + identity)
    factor_below = solve_rows(factor_diag, below_total)
    return (factor_diag, factor_below)


def solution(mesh):
    in_specs = (
        P(("user", "item"), None),
        P("user", "item", None),
        P("user", "item"),
        P("user", "item"),
    )
    out_specs = (P(), P("item", None))
    return jax.shard_map(
        on_device, mesh=mesh, in_specs=in_specs, out_specs=out_specs, check_vma=False
    )
```

profile of v0, /device:TPU:1, one launch (start us, length us, event | category | flops | bytes accessed | tf_op | source)
XLA Modules:
  0.0 236.8 jit_solution(12688199129750226342)
XLA Ops:
  7.2 0.0 copy-start
  7.2 0.0 all-reduce.4.cloned.1.call-start
  7.2 38.7 %all_gather.3 = bf16[512,256]{1,0:T(8,128)(2,1)S(1)} all-gather(bf16[16,256]{1,0:T(8,128)(2,1)} %param.4), channel_id=1, replica_groups=mesh['user'=16,'item'=32] {'item'}, dimensions={0}, use_global_device_ids=true | all-gather | bytes 270336 | tf_op jit(solution)/shard_map/all_gather | solution.py:18
  45.9 1.0 fusion.19
  46.9 0.0 copy-done
  46.9 0.4 fusion.4
  48.0 0.0 copy-start.3
  48.0 0.6 copy-done.3
  48.6 1.1 fusion
  49.7 1.3 copy.9
  51.0 0.0 all-reduce.4.cloned.1.call-update
  51.1 112.9 %all-reduce.4.cloned.1.call-done = (f32[256,256]{1,0:T(8,128)}, f32[1024,256]{1,0:T(8,128)}) async-done(((f32[256,256]{1,0:T(8,128)}, f32[1024,256]{1,0:T(8,128)}), (f32[256,256]{1,0:T(8,128)}, f32[1024,256]{1,0:T(8,128)})) %all-reduce.4.cloned.1.call-update) | async-done | bytes 1310736 | tf_op jit(solution)/shard_map/psum | solution.py:32
  163.9 1.0 select_add_fusion
  164.9 0.0 copy-start.2
  164.9 0.1 copy.8
  165.0 0.8 copy-done.2
  165.9 11.7 %cholesky.49 = f32[128,128]{1,0:T(8,128)S(1)} custom-call(f32[128,128]{1,0:T(8,128)S(1)} %cholesky.115), custom_call_target="Cholesky" | custom-call | tf_op jit(solution)/shard_map/jit(cholesky)/cholesky | solution.py:33
  177.7 9.8 %custom-call.14 = f32[1,128,128]{1,2,0:T(8,128)S(1)} custom-call(f32[1,128,128]{2,1,0:T(8,128)S(1)} %get-tuple-element.31), custom_call_target="InvertDiagBlocksLowerTriangular" | custom-call | tf_op jit(solution)/shard_map/jit(cholesky)/cholesky | solution.py:33
  187.5 0.2 constant_dynamic-update-slice_fusion.1
  187.7 0.0 copy-start.1
  187.7 0.3 convolution_subtract_fusion.1
  188.0 11.8 %cholesky.103 = f32[128,128]{1,0:T(8,128)S(1)} custom-call(f32[128,128]{1,0:T(8,128)S(1)} %convolution_subtract_fusion.1), custom_call_target="Cholesky" | custom-call | tf_op jit(solution)/shard_map/jit(cholesky)/cholesky | solution.py:33
  199.9 0.6 compare_reduce_fusion
  201.8 0.7 fusion.7
  202.5 0.1 triangular_solve.43
  202.6 4.0 %while.1 = (s32[]{:T(128)}, f32[256,256]{1,0:T(8,128)S(1)}, s32[2,2]{1,0:T(2,128)S(1)}, f32[2,128,128]{2,1,0:T(8,128)S(1)}, s32[]{:T(128)}) while((s32[]{:T(128)}, f32[256,256]{1,0:T(8,128)S(1)}, s32[2,2]{1,0:T(2,128)S(1)}, f32[2,128,128]{2,1,0:T(8,128)S(1)}, s32[]{:T(128)}) %tuple.30), condition=%wide.while_cond, body=%wide.while_body.sunk | while | flops 2 | bytes 131189 | solution.py:12
  202.6 0.6 fusion.28
  203.2 1.4 bitcast_dynamic-update-slice_fusion.2
  204.6 0.6 fusion.28
  205.2 1.4 bitcast_dynamic-update-slice_fusion.2
  206.6 19.7 %custom-call.15 = f32[2,128,128]{1,2,0:T(8,128)S(1)} custom-call(f32[2,128,128]{2,1,0:T(8,128)S(1)} %get-tuple-element.9), custom_call_target="InvertDiagBlocksLowerTriangular" | custom-call | tf_op jit(solution)/shard_map/triangular_solve | solution.py:12
  226.3 0.0 copy-done.1
  226.3 0.6 fusion.2
  226.9 1.0 convolution_subtract_fusion
  227.9 0.6 fusion.8
  228.5 0.1 pad_maximum_fusion
  228.6 1.3 copy.10
  (10 shorter events, 0.2 us)
Async XLA Ops:
  7.2 39.7 %copy-start = (bf16[512,7,128]{2,0,1:T(8,128)(2,1)S(1)}, bf16[512,7,128]{2,0,1:T(8,128)(2,1)}, u32[]{:S(2)}) copy-start(bf16[512,7,128]{2,0,1:T(8,128)(2,1)} %param.5) | copy-start | bytes 2752516
  7.2 156.7 %all-reduce.4.cloned.1.call-start = ((), (), s32[]{:S(2)}) async-start(), calls=%async_computation | async-start | bytes 2621440 | tf_op jit(solution)/shard_map/psum | solution.py:32
  48.0 0.7 copy-start.3
  164.9 1.0 copy-start.2
  187.7 38.6 %copy-start.1 = (f32[1024,256]{1,0:T(8,128)S(1)}, f32[1024,256]{1,0:T(8,128)}, u32[]{:S(2)}) copy-start(f32[1024,256]{1,0:T(8,128)} %get-tuple-element.23) | copy-start | bytes 3145732
Sparse Core Ops, SparseCore 0:
  51.2 112.7 all-reduce.3
where the time goes:
time: 237 us
  waiting for transfers between devices  113 us (48%)
  other arithmetic  55.6 us (23%)
  blocking collectives  38.7 us (16%)
  between operations  16.1 us (7%)
  local copies, waits for them, and re-layouts  8.23 us (3%)
  matrix products  5.2 us (2%)
    psum x1, waiting for transfers between devices, on_device(): diag_total, below_total = lax.psum((diag_part, below_part), 'user')  113 us
    all_gather x1, blocking collectives, on_device(): gathered = lax.all_gather(panel_users, 'item', axis=0, tiled=True)  38.7 us
    another operation x6, other arithmetic, on_device(): factor_diag = jnp.linalg.cholesky(diag_total + identity)  34.1 us
    another operation x4, other arithmetic, solve_rows(): lax.linalg.triangular_solve(factor_diag, rows, left_side=False, lower=Tru...  20.5 us
  transfers between devices with their start and end apart: 1, of which 1 were waited for; matrix products, arithmetic and copies ran while one was open for 0% of the time, Pallas kernels for 0%

commit v1 on v0

v1 whole, which is shorter than its diff:
```python
import functools

import jax
import jax.numpy as jnp
from jax import lax
from jax.sharding import PartitionSpec as P
import jax.experimental.pallas as pl
import jax.experimental.pallas.tpu as pltpu

BLOCK = 128
PANEL = 256
BLK_DEV = 8
SIDE = 4
DEPTH = 16
SHARE = 16
NB = 16
MESH = pl.DeviceIdType.MESH
FAR_FIRST_Z = (8, 7, 9, 6, 10, 5, 11, 4, 12, 3, 13, 2, 14, 1, 15)
FAR_FIRST_XY = sorted(
    ((dy, dx) for dy in range(SIDE) for dx in range(SIDE) if dy or dx),
    key=lambda d: -(min(d[0], SIDE - d[0]) + min(d[1], SIDE - d[1])),
)
FAR_FIRST_SIDE = (2, 1, 3)


def split3(x):
    high = x.astype(jnp.bfloat16)
    rest = x - high.astype(jnp.float32)
    middle = rest.astype(jnp.bfloat16)
    low = (rest - middle.astype(jnp.float32)).astype(jnp.bfloat16)
    return high, middle, low


def eliminate(rows, sub, lane):
    tiles = len(rows)
    count = 8 * tiles
    columns = [
        [jnp.broadcast_to(rows[k][0][:, t : t + 1], (8, 128)) for k in range(tiles)] for t in range(count)
    ]
    inverse = [jnp.where(lane == sub + 8 * k, 1.0, 0.0).astype(jnp.float32) for k in range(tiles)]
    pivots = [None] * tiles
    for t in range(count):
        kt, s = divmod(t, 8)
        here = columns[t][kt]
        pivots[kt] = here if s == 0 else jnp.where(sub == s, here, pivots[kt])
        if t == count - 1:
            break
        reciprocal = 1.0 / jnp.broadcast_to(here[s : s + 1, :], (8, 128))
        below = {k: columns[t][k] for k in range(kt + 1, tiles)}
        if s < 7:
            below[kt] = jnp.where(sub > s, here, 0.0)
        for j in range(t + 1, count):
            pivot_row = jnp.broadcast_to(columns[j][kt][s : s + 1, :], (8, 128))
            for k in below:
                columns[j][k] = columns[j][k] - (below[k] * pivot_row) * reciprocal
        scaled = {k: below[k] * reciprocal for k in below}
        for h in range(len(rows[0])):
            pivot_row = jnp.broadcast_to(rows[kt][h][s : s + 1, :], (8, 128))
            for k in below:
                rows[k][h] = rows[k][h] - scaled[k] * pivot_row
        pivot_row = jnp.broadcast_to(inverse[kt][s : s + 1, :], (8, 128))
        for k in below:
            inverse[k] = inverse[k] - scaled[k] * pivot_row
    return rows, inverse, pivots


def factor_step(step, work_ref, upper_ref):
    tiles = NB // 8
    sub = lax.broadcasted_iota(jnp.int32, (8, 128), 0)
    lane = lax.broadcasted_iota(jnp.int32, (8, 128), 1)
    rows = [[work_ref[8 * k : 8 * k + 8, 128 * h : 128 * h + 128] for h in range(2)] for k in range(tiles)]
    rows, inverse, pivots = eliminate(rows, sub, lane)
    scale = [lax.rsqrt(p) for p in pivots]
    upper = jnp.concatenate(
        [jnp.concatenate([rows[k][h] * scale[k] for h in range(2)], 1) for k in range(tiles)], 0
    )
    inverse = jnp.concatenate([inverse[k] * scale[k] for k in range(tiles)], 0)
    inverse = jnp.concatenate([inverse, inverse], 1)
    col = lax.broadcasted_iota(jnp.int32, (NB, PANEL), 1)
    row = lax.broadcasted_iota(jnp.int32, (NB, PANEL), 0)
    left = PANEL - NB * step
    trailing = (col >= NB) & (col < left)
    done = jnp.where(col < NB, inverse, upper)
    into = jnp.where(trailing, upper, 0.0)
    upper_ref[pl.ds(pl.multiple_of(step * NB, NB), NB), :] = jnp.where((col >= row) & (col < left), upper, 0.0)
    dh, dm, dl = split3(done)
    ih, im, il = split3(into)
    product = lax.dot_general(
        jnp.concatenate([ih, ih, im, ih, im, il], 0),
        jnp.concatenate([dh, dm, dh, dl, dm, dh], 0),
        (((0,), (0,)), ((), ())),
        preferred_element_type=jnp.float32,
    )
    wide = lax.broadcasted_iota(jnp.int32, (PANEL - NB, PANEL), 1)
    new = jnp.where(wide < NB, 0.0, work_ref[NB:, :]) - product[NB:, :]
    work_ref[0 : PANEL - NB, :] = pltpu.roll(new, PANEL - NB, 1)
    work_ref[PANEL - NB :, :] = pltpu.roll(jnp.where(trailing, 0.0, done), PANEL - NB, 1)


def factor_steps(first, last, work_ref, upper_ref):
    def body(step, carry):
        factor_step(step, work_ref, upper_ref)
        return carry

    lax.fori_loop(first, last, body, 0)


def turn_back(upper_ref):
    def body(step, carry):
        rows = pl.ds(pl.multiple_of(step * NB, NB), NB)
        upper_ref[rows, :] = pltpu.roll(upper_ref[rows, :], step * NB, 1)
        return carry

    lax.fori_loop(0, PANEL // NB, body, 0)


def gram_kernel(
    panel_ref, values_ref, list_ref, count_ref, upper_ref, inverse_ref, sum_ref,
    users, values, turned, diag, diag_in, part, in1, sum1, in2,
    values_sem, z_send, z_recv, core_send, core_recv, ds_send, ds_recv, dg_send, dg_recv,
    s1_send, s1_recv, s2_send, s2_recv, s3_send, s3_recv, s4_send, s4_recv,
):
    user = lax.axis_index("user")
    item = lax.axis_index("item")
    y, x = user // SIDE, user % SIDE
    z, core = item // 2, item % 2
    other = 1 - core

    def at_xy(dy, dx):
        return ((y + dy) % SIDE) * SIDE + (x + dx) % SIDE

    def at_z(dz):
        return (z + dz) % DEPTH

    z_ids = [(user, at_z(d) * 2 + core) for d in FAR_FIRST_Z]
    xy_ids = [(at_xy(*d), item) for d in FAR_FIRST_XY]
    core_id = (user, z * 2 + other)

    def remote(src, dst, send, recv, device):
        return pltpu.make_async_remote_copy(
            src_ref=src, dst_ref=dst, send_sem=send, recv_sem=recv, device_id=device, device_id_type=MESH
        )

    barrier = pltpu.get_barrier_semaphore()
    for device in z_ids + xy_ids + [core_id]:
        pl.semaphore_signal(barrier, inc=1, device_id=device, device_id_type=MESH)

    loads = [
        pltpu.make_async_copy(
            values_ref.at[:, :, c], values.at[c, pl.ds(0, BLK_DEV - 1)], values_sem.at[c]
        )
        for c in range(2)
    ]
    for load in loads:
        load.start()
    for c in range(2):
        values[c, BLK_DEV - 1] = jnp.zeros((DEPTH, SHARE, BLOCK), jnp.bfloat16)
    users[core, z] = panel_ref[...]

    pl.semaphore_wait(barrier, len(z_ids) + len(xy_ids) + 1)

    z_copies = [
        remote(users.at[core, z], users.at[core, z], z_send.at[k], z_recv.at[k], device)
        for k, device in enumerate(z_ids)
    ]
    for copy in z_copies:
        copy.start()

    for load in loads:
        load.wait()
    used = count_ref[0, 0]
    for b in range(BLK_DEV):
        slot = jnp.int32(BLK_DEV - 1)
        for k in range(BLK_DEV - 1):
            slot = jnp.where((list_ref[0, k] == b) & (k < used), k, slot)
        for c in range(2):
            block = values[c, slot].reshape(DEPTH * SHARE, BLOCK)
            turned[c, pl.ds(b * BLOCK, BLOCK), :] = block.T

    for copy in z_copies:
        copy.wait()
    core_copy = remote(users.at[core], users.at[core], core_send, core_recv, core_id)
    core_copy.start()

    def partial(c):
        rows = users[c].reshape(DEPTH * SHARE, PANEL)
        return lax.dot_general(rows, rows, (((0,), (0,)), ((), ())), preferred_element_type=jnp.float32)

    diag[...] = partial(core)
    below = jnp.dot(
        turned[core], users[core].reshape(DEPTH * SHARE, PANEL), preferred_element_type=jnp.float32
    )
    part[0] = below[:, :BLOCK]
    part[1] = below[:, BLOCK:]
    core_copy.wait()
    diag[...] += partial(other)

    def diag_rows(device_user):
        return pl.ds(pl.multiple_of(device_user * SHARE, SHARE), SHARE)

    ds_copies = [
        remote(diag.at[diag_rows(d[0])], diag_in.at[user], ds_send.at[k], ds_recv.at[k], d)
        for k, d in enumerate(xy_ids)
    ]
    for copy in ds_copies:
        copy.start()
    diag_in[user] = diag[diag_rows(user), :]

    below = jnp.dot(
        turned[other], users[other].reshape(DEPTH * SHARE, PANEL), preferred_element_type=jnp.float32
    )
    part[0] += below[:, :BLOCK]
    part[1] += below[:, BLOCK:]

    along = (
        [((at_xy(0, d), item), (x + d) % SIDE) for d in FAR_FIRST_SIDE],
        [((at_xy(d, 0), item), (y + d) % SIDE) for d in FAR_FIRST_SIDE],
    )
    place = (x, y)
    big, small = BLK_DEV * BLOCK // SIDE, BLK_DEV * BLOCK // SIDE**2

    def big_rows(i):
        return pl.ds(pl.multiple_of(i * big, big), big)

    def small_rows(i):
        return pl.ds(pl.multiple_of(i * small, small), small)

    s1_copies = [
        remote(part.at[h, big_rows(there)], in1.at[h, k], s1_send.at[h, k], s1_recv.at[h, k], device)
        for k in range(SIDE - 1)
        for h in range(2)
        for device, there in [along[h][k]]
    ]
    for copy in s1_copies:
        copy.start()

    for copy in ds_copies:
        copy.wait()
    total = diag_in[0]
    for k in range(1, SIDE * SIDE):
        total = total + diag_in[k]
    row = lax.broadcasted_iota(jnp.int32, (SHARE, PANEL), 0) + user * SHARE
    col = lax.broadcasted_iota(jnp.int32, (SHARE, PANEL), 1)
    inverse_ref[diag_rows(user), :] = total + jnp.where(row == col, 0.5, 0.0)
    dg_copies = [
        remote(
            inverse_ref.at[diag_rows(user)], inverse_ref.at[diag_rows(user)], dg_send.at[k], dg_recv.at[k], d
        )
        for k, d in enumerate(xy_ids)
    ]
    for copy in dg_copies:
        copy.start()

    for copy in s1_copies:
        copy.wait()
    for h in range(2):
        sum1[h] = part[h, big_rows(place[h]), :] + in1[h, 0] + in1[h, 1] + in1[h, 2]
    s2_copies = [
        remote(sum1.at[h, small_rows(there)], in2.at[h, k], s2_send.at[h, k], s2_recv.at[h, k], device)
        for k in range(SIDE - 1)
        for h in range(2)
        for device, there in [along[1 - h][k]]
    ]
    for copy in s2_copies:
        copy.start()

    for copy in dg_copies:
        copy.wait()
    for copy in s2_copies:
        copy.wait()
    mine = (x * SIDE + y, y * SIDE + x)
    for h in range(2):
        sum_ref[h, small_rows(mine[h]), :] = (
            sum1[h, small_rows(place[1 - h]), :] + in2[h, 0] + in2[h, 1] + in2[h, 2]
        )
    s3_copies = [
        remote(
            sum_ref.at[h, small_rows(mine[h])], sum_ref.at[h, small_rows(mine[h])],
            s3_send.at[h, k], s3_recv.at[h, k], along[1 - h][k][0],
        )
        for k in range(SIDE - 1)
        for h in range(2)
    ]
    for copy in s3_copies:
        copy.start()
    factor_steps(0, 5, inverse_ref, upper_ref)
    for copy in s3_copies:
        copy.wait()
    s4_copies = [
        remote(
            sum_ref.at[h, big_rows(place[h])], sum_ref.at[h, big_rows(place[h])],
            s4_send.at[h, k], s4_recv.at[h, k], along[h][k][0],
        )
        for k in range(SIDE - 1)
        for h in range(2)
    ]
    for copy in s4_copies:
        copy.start()
    factor_steps(5, PANEL // NB, inverse_ref, upper_ref)
    turn_back(upper_ref)
    for copy in s4_copies:
        copy.wait()


def solve_kernel(upper_ref, inverse_ref, sum_ref, diag_ref, below_ref):
    diag_ref[...] = upper_ref[...].T
    rows = jnp.concatenate([sum_ref[0], sum_ref[1]], 1)
    below_ref[...] = lax.dot_general(
        rows, inverse_ref[...], (((1,), (1,)), ((), ())),
        precision=lax.Precision.HIGHEST, preferred_element_type=jnp.float32,
    )


def on_device(panel_users, block_values, block_list, block_count):
    f32, bf16 = jnp.float32, jnp.bfloat16
    rows = BLK_DEV * BLOCK
    big, small = rows // SIDE, rows // SIDE**2
    slots = block_values.shape[1]
    values = block_values.transpose(1, 0, 2).reshape(slots, DEPTH, 2, SHARE, BLOCK)
    vmem = pl.BlockSpec(memory_space=pltpu.VMEM)
    smem = pl.BlockSpec(memory_space=pltpu.SMEM)
    sems = pltpu.SemaphoreType.DMA
    xy = SIDE * SIDE - 1
    upper, inverse, total = pl.pallas_call(
        gram_kernel,
        out_shape=[
            jax.ShapeDtypeStruct((PANEL, PANEL), f32),
            jax.ShapeDtypeStruct((PANEL, PANEL), f32),
            jax.ShapeDtypeStruct((2, rows, BLOCK), f32),
        ],
        in_specs=[vmem, pl.BlockSpec(memory_space=pl.ANY), smem, smem],
        out_specs=[vmem, vmem, vmem],
        scratch_shapes=[
            pltpu.VMEM((2, DEPTH, SHARE, PANEL), bf16),
            pltpu.VMEM((2, BLK_DEV, DEPTH, SHARE, BLOCK), bf16),
            pltpu.VMEM((2, rows, 2 * BLOCK), bf16),
            pltpu.VMEM((PANEL, PANEL), f32),
            pltpu.VMEM((SIDE * SIDE, SHARE, PANEL), f32),
            pltpu.VMEM((2, rows, BLOCK), f32),
            pltpu.VMEM((2, SIDE - 1, big, BLOCK), f32),
            pltpu.VMEM((2, big, BLOCK), f32),
            pltpu.VMEM((2, SIDE - 1, small, BLOCK), f32),
            sems((2,)),
            sems((DEPTH - 1,)),
            sems((DEPTH - 1,)),
            sems,
            sems,
            sems((xy,)),
            sems((xy,)),
            sems((xy,)),
            sems((xy,)),
        ]
        + [sems((2, SIDE - 1))] * 8,
        compiler_params=pltpu.CompilerParams(
            collective_id=0, has_side_effects=True, vmem_limit_bytes=32 << 20
        ),
        name="gram",
    )(panel_users, values, block_list, block_count)
    return pl.pallas_call(
        solve_kernel,
        out_shape=[jax.ShapeDtypeStruct((PANEL, PANEL), f32), jax.ShapeDtypeStruct((rows, PANEL), f32)],
        in_specs=[vmem] * 3,
        out_specs=[vmem] * 2,
        compiler_params=pltpu.CompilerParams(vmem_limit_bytes=32 << 20),
        name="solve",
    )(upper, inverse, total)


def solution(mesh):
    in_specs = (
        P(("user", "item"), None),
        P("user", "item", None),
        P("user", "item"),
        P("user", "item"),
    )
    out_specs = (P(), P("item", None))
    return jax.shard_map(
        on_device, mesh=mesh, in_specs=in_specs, out_specs=out_specs, check_vma=False
    )
```

time: 237 us -> 61.3 us (0.26)
  waiting for transfers between devices: 113 us -> 0 us
  Pallas kernels: 0 us -> 57.3 us
  other arithmetic: 55.6 us -> 0 us
  blocking collectives: 38.7 us -> 0 us
  between operations: 16.1 us -> 1.3 us
  local copies, waits for them, and re-layouts: 8.23 us -> 2.52 us
  matrix products: 5.2 us -> 0 us
    psum x1 -> x0, waiting for transfers between devices: 113 us -> none  [on_device(): diag_total, below_total = lax.psum((diag_part, below_part), 'user')]
    pallas_call x0 -> x2, Pallas kernels: none -> 57.3 us  [the longest x1 55.3 us: on_device(): pl.pallas_call(gram_kernel, out_shape=[jax.ShapeDtypeStruct((PANEL, PANEL...]
    another operation x10 -> x0, other arithmetic: 54.6 us -> none  [the longest x6 34.1 us: on_device(): factor_diag = jnp.linalg.cholesky(diag_total + identity)]
    all_gather x1 -> x0, blocking collectives: 38.7 us -> none  [on_device(): gathered = lax.all_gather(panel_users, 'item', axis=0, tiled=True)]
    another operation x9 -> x0, local copies, waits for them, and re-layouts: 4.02 us -> none
    another operation x5 -> x0, matrix products: 2.7 us -> none  [the longest x3 2.23 us: solve_rows(): lax.linalg.triangular_solve(factor_diag, rows, left_side=False, lower=Tru...]
    dot_general x3 -> x0, matrix products: 2.5 us -> none  [the longest x1 1.09 us: on_device(): jnp.einsum('kb,kcp->bcp', chosen.astype(jnp.float32), product, precision=...]
  transfers between devices with their start and end apart: 1 -> 0, of which waited for: 1 -> 0; matrix products, arithmetic and copies ran while one was open for 0% -> 0% of each run, Pallas kernels for 0% -> 0%
where the time goes in v1:
time: 61.3 us; the launch traced here: 61.1 us
  Pallas kernels  57.3 us (93%)
  local copies, waits for them, and re-layouts  2.52 us (4%)
  between operations  1.3 us (2%)
    pallas_call x1, Pallas kernels, on_device(): pl.pallas_call(gram_kernel, out_shape=[jax.ShapeDtypeStruct((PANEL, PANEL...  55.3 us
    unnamed x6, local copies, waits for them, and re-layouts  2.52 us
    pallas_call x1, Pallas kernels, on_device(): pl.pallas_call(solve_kernel, out_shape=[jax.ShapeDtypeStruct((PANEL, PANE...  2.02 us

profile of v1, /device:TPU:1, one launch (start us, length us, event | category | flops | bytes accessed | tf_op | source)
XLA Modules:
  0.0 61.1 jit_solution(9851100554271811057)
XLA Ops:
  1.3 0.0 copy-start.2
  1.3 0.6 %copy-done.2 = s32[1,7]{1,0:T(1,128)S(1)} copy-done((s32[1,7]{1,0:T(1,128)S(1)}, s32[1,7]{1,0:T(1,128)}, u32[]{:S(2)}) %copy-start.2) | copy-done | bytes 52
  1.9 0.0 copy-start
  1.9 1.2 %copy-done = bf16[512,7,128]{2,0,1:T(8,128)(2,1)S(1)} copy-done((bf16[512,7,128]{2,0,1:T(8,128)(2,1)S(1)}, bf16[512,7,128]{2,0,1:T(8,128)(2,1)}, u32[]{:S(2)}) %copy-start) | copy-done | bytes 917528
  3.1 0.0 copy-start.1
  3.1 0.7 %copy-done.1 = bf16[16,256]{1,0:T(8,128)(2,1)S(1)} copy-done((bf16[16,256]{1,0:T(8,128)(2,1)S(1)}, bf16[16,256]{1,0:T(8,128)(2,1)}, u32[]{:S(2)}) %copy-start.1) | copy-done | bytes 8216
  3.8 55.3 %gram.1 = (f32[256,256]{1,0:T(8,128)S(1)}, f32[256,256]{1,0:T(8,128)S(1)}, f32[2,1024,128]{2,1,0:T(8,128)S(1)}) custom-call(bf16[16,256]{1,0:T(8,128)(2,1)S(1)} %copy-done.1, bf16[7,16,2,16,128]{4,3,2,1,0:T(8,128)(2,1)S(1)} %bitcast.3, s32[1,7]{1,0:T(1,128)S(1)} %copy-done.2, s32[1,1]{1,0:T(1,128)S(6)} %copy.6.count_ref), custom_call_target="tpu_custom_call" | custom-call | tf_op jit(solution)/shard_map/gram/pallas_call | solution.py:324
  59.1 2.0 %solve.1 = (f32[256,256]{1,0:T(8,128)}, f32[1024,256]{1,0:T(8,128)}) custom-call(f32[256,256]{1,0:T(8,128)S(1)} %get-tuple-element.5.upper_ref, f32[256,256]{1,0:T(8,128)S(1)} %get-tuple-element.6.inverse_ref, f32[2,1024,128]{2,1,0:T(8,128)S(1)} %get-tuple-element.7.sum_ref), custom_call_target="tpu_custom_call" | custom-call | tf_op jit(solution)/shard_map/solve/pallas_call | solution.py:359
Async XLA Ops:
  1.3 0.7 %copy-start.2 = (s32[1,7]{1,0:T(1,128)S(1)}, s32[1,7]{1,0:T(1,128)}, u32[]{:S(2)}) copy-start(s32[1,7]{1,0:T(1,128)} %list_ref.1) | copy-start | bytes 88
  1.9 1.2 %copy-start = (bf16[512,7,128]{2,0,1:T(8,128)(2,1)S(1)}, bf16[512,7,128]{2,0,1:T(8,128)(2,1)}, u32[]{:S(2)}) copy-start(bf16[512,7,128]{2,0,1:T(8,128)(2,1)} %param.5) | copy-start | bytes 2752516
  3.1 0.7 %copy-start.1 = (bf16[16,256]{1,0:T(8,128)(2,1)S(1)}, bf16[16,256]{1,0:T(8,128)(2,1)}, u32[]{:S(2)}) copy-start(bf16[16,256]{1,0:T(8,128)(2,1)} %panel_ref.1) | copy-start | bytes 24580

commit v2 on v0

v2 whole, which is shorter than its diff:
```python
import jax
import jax.numpy as jnp
from jax import lax
from jax.sharding import PartitionSpec as P
import jax.experimental.pallas as pl
import jax.experimental.pallas.tpu as pltpu

BLOCK = 128
PANEL = 256
BLK_DEV = 8
ROWS = BLK_DEV * BLOCK
SIDE = 4
DEPTH = 16
SHARE = 16
TILE = 8
NB = 32
STORES = 4
PIECES = 4
MESH = pl.DeviceIdType.MESH
FAR_FIRST_Z = (8, 7, 9, 6, 10, 5, 11, 4, 12, 3, 13, 2, 14, 1, 15)
FAR_FIRST_XY = sorted(
    ((dy, dx) for dy in range(SIDE) for dx in range(SIDE) if dy or dx),
    key=lambda d: -(min(d[0], SIDE - d[0]) + min(d[1], SIDE - d[1])),
)
FAR_FIRST_SIDE = (2, 1, 3)
ORDER = (
    ("sum", 0), ("sum", 1), ("diag", 0), ("factor", 0), ("sum", 2), ("factor", 1), ("sum", 3), ("pass", 0), ("factor", 2),
    ("pass", 1), ("factor", 3), ("pass", 2), ("factor", 4), ("pass", 3), ("factor", 5), ("factor", 6), ("factor", 7),
)


def split3(x):
    high = x.astype(jnp.bfloat16)
    rest = x - high.astype(jnp.float32)
    middle = rest.astype(jnp.bfloat16)
    low = (rest - middle.astype(jnp.float32)).astype(jnp.bfloat16)
    return high, middle, low


def eliminate(rows, inverse, start, count):
    left = rows.shape[0]
    columns = jnp.stack([jnp.broadcast_to(rows[:, start + t : start + t + 1], (left, BLOCK)) for t in range(count)])
    tile_sub = lax.broadcasted_iota(jnp.int32, (8, BLOCK), 0)
    rows_done, inverse_done, pivots = [], [], None
    for t in range(count):
        s = t % 8
        here = columns[0]
        pivots = jnp.where(tile_sub == s, here[:8], pivots) if s else here[:8]
        reciprocal = 1.0 / here[s : s + 1]
        below = jnp.where(lax.broadcasted_iota(jnp.int32, (left, BLOCK), 0) > s, here, 0.0)
        if t < count - 1:
            columns = columns[1:] - (below[None] * columns[1:, s : s + 1]) * reciprocal[None]
        scaled = below * reciprocal
        rows = rows - jnp.concatenate([scaled, scaled], 1) * rows[s : s + 1]
        inverse = inverse - scaled * inverse[s : s + 1]
        if s == 7:
            scale = lax.rsqrt(pivots)
            rows_done.append(rows[:8] * jnp.concatenate([scale, scale], 1))
            inverse_done.append(inverse[:8] * scale)
            left -= 8
            if left:
                rows, inverse, columns = rows[8:], inverse[8:], columns[:, 8:]
    return rows_done, inverse_done, rows, inverse


def factor_step(step, work_ref, upper_ref):
    start, stop = NB * step, NB * (step + 1)
    rows = work_ref[start:stop, :]
    lane = lax.broadcasted_iota(jnp.int32, (NB, BLOCK), 1)
    sub = lax.broadcasted_iota(jnp.int32, (NB, BLOCK), 0)
    inverse = jnp.where(lane == sub + start % BLOCK, 1.0, 0.0).astype(jnp.float32)
    rows1, inverse1, rows, inverse = eliminate(rows, inverse, start, NB // 2)
    rows2, inverse2, _, _ = eliminate(rows, inverse, start + NB // 2, NB // 2)
    upper = jnp.concatenate(rows1 + rows2, 0)
    inverse = jnp.concatenate(inverse1 + inverse2, 0)
    col = lax.broadcasted_iota(jnp.int32, (NB, PANEL), 1)
    row = lax.broadcasted_iota(jnp.int32, (NB, PANEL), 0)
    done = jnp.where((col >= start) & (col < stop), jnp.concatenate([inverse, inverse], 1), upper)
    upper_ref[start:stop, :] = jnp.where(col >= row + start, upper, 0.0)
    work_ref[start:stop, :] = jnp.where(col < stop, done, 0.0)
    if stop == PANEL:
        return
    base = BLOCK * (stop // BLOCK)
    dh, dm, dl = split3(done)
    ih, im, il = split3(upper[:, base:])
    product = lax.dot_general(
        jnp.concatenate([ih, ih, im, ih, im, il], 0),
        jnp.concatenate([dh, dm, dh, dl, dm, dh], 0),
        (((0,), (0,)), ((), ())),
        preferred_element_type=jnp.float32,
    )
    wide = lax.broadcasted_iota(jnp.int32, (PANEL - stop, PANEL), 1)
    kept = jnp.where((wide >= start) & (wide < stop), 0.0, work_ref[stop:, :])
    work_ref[stop:, :] = kept - product[stop - base :, :]


def gram_kernel(
    panel_ref, values_ref, list_ref, count_ref, diag_out, below_out,
    users, values, turned, slot_list, slot_count, diag, diag_in, work, part, in1, sum1, in2, total, upper_ref, below_ref,
    load_sem, store_sem, z_send, z_recv, core_send, core_recv, ds_send, ds_recv, dg_send, dg_recv, half_sem,
    s1_send, s1_recv, s2_send, s2_recv, s3_send, s3_recv, s4_send, s4_recv,
):
    user = lax.axis_index("user")
    item = lax.axis_index("item")
    y, x = user // SIDE, user % SIDE
    z, core = item // 2, item % 2
    other = 1 - core

    def at_xy(dy, dx):
        return ((y + dy) % SIDE) * SIDE + (x + dx) % SIDE

    z_ids = [(user, ((z + d) % DEPTH) * 2 + core) for d in FAR_FIRST_Z]
    xy_ids = [(at_xy(*d), item) for d in FAR_FIRST_XY]
    core_id = (user, z * 2 + other)

    def remote(src, dst, send, recv, device):
        return pltpu.make_async_remote_copy(
            src_ref=src, dst_ref=dst, send_sem=send, recv_sem=recv, device_id=device, device_id_type=MESH
        )

    def start(copies):
        for copy in copies:
            copy.start()

    def wait(copies):
        for copy in copies:
            copy.wait()

    barrier = pltpu.get_barrier_semaphore()
    for device in z_ids + xy_ids + [core_id]:
        pl.semaphore_signal(barrier, inc=1, device_id=device, device_id_type=MESH)

    own_load = pltpu.make_async_copy(panel_ref, users.at[core, z], load_sem.at[0])
    loads = [
        pltpu.make_async_copy(list_ref, slot_list, load_sem.at[1]),
        pltpu.make_async_copy(count_ref, slot_count, load_sem.at[2]),
    ] + [
        pltpu.make_async_copy(values_ref.at[:, :, c], values.at[c, pl.ds(0, BLK_DEV - 1)], load_sem.at[3 + c])
        for c in range(2)
    ]
    start([own_load] + loads)
    for c in range(2):
        values[c, BLK_DEV - 1] = jnp.zeros((DEPTH, SHARE, BLOCK), jnp.bfloat16)
    own_load.wait()
    pl.semaphore_wait(barrier, len(z_ids) + len(xy_ids) + 1)

    z_copies = [
        remote(users.at[core, z], users.at[core, z], z_send.at[k], z_recv.at[k], device)
        for k, device in enumerate(z_ids)
    ]
    start(z_copies)
    core_copies = []
    for k, d in enumerate((0,) + FAR_FIRST_Z):
        came_from = (z + DEPTH - d) % DEPTH
        core_copies.append(
            remote(users.at[core, came_from], users.at[core, came_from], core_send.at[k], core_recv.at[k], core_id)
        )
    core_copies[0].start()

    wait(loads)
    used = slot_count[0, 0]
    for b in range(BLK_DEV):
        slot = jnp.int32(BLK_DEV - 1)
        for k in range(BLK_DEV - 1):
            slot = jnp.where((slot_list[0, k] == b) & (k < used), k, slot)
        for c in range(2):
            block = values[c, slot].reshape(DEPTH * SHARE, BLOCK)
            turned[pl.ds(b * BLOCK, BLOCK), pl.ds(c * DEPTH * SHARE, DEPTH * SHARE)] = block.T

    for k in reversed(range(DEPTH - 1)):
        z_copies[k].wait_recv()
        core_copies[k + 1].start()
    wait(core_copies)
    for copy in z_copies:
        copy.wait_send()

    along = (
        [((at_xy(0, d), item), (x + d) % SIDE) for d in FAR_FIRST_SIDE],
        [((at_xy(d, 0), item), (y + d) % SIDE) for d in FAR_FIRST_SIDE],
    )
    place = (x, y)
    piece = ROWS // PIECES
    big, small = piece // SIDE, piece // SIDE**2

    def big_rows(q, i):
        return pl.ds(pl.multiple_of(q * piece + i * big, big), big)

    def small_rows(q, i):
        return pl.ds(pl.multiple_of(q * piece + i * small, small), small)

    def own_rows(q, h):
        return small_rows(q, place[h] * SIDE + place[1 - h])

    pairs = [(k, h) for k in range(SIDE - 1) for h in range(2)]
    s1 = [
        [
            remote(
                part.at[h, big_rows(q, along[h][k][1])], in1.at[q, h, k],
                s1_send.at[q, h, k], s1_recv.at[q, h, k], along[h][k][0],
            )
            for k, h in pairs
        ]
        for q in range(PIECES)
    ]
    s2 = [
        [
            remote(
                sum1.at[q, h, pl.ds(pl.multiple_of(along[1 - h][k][1] * small, small), small)], in2.at[q, h, k],
                s2_send.at[q, h, k], s2_recv.at[q, h, k], along[1 - h][k][0],
            )
            for k, h in pairs
        ]
        for q in range(PIECES)
    ]
    s3 = [
        [
            remote(
                total.at[h, own_rows(q, h)], total.at[h, own_rows(q, h)],
                s3_send.at[q, h, k], s3_recv.at[q, h, k], along[1 - h][k][0],
            )
            for k, h in pairs
        ]
        for q in range(PIECES)
    ]
    s4 = [
        [
            remote(
                total.at[h, big_rows(q, place[h])], total.at[h, big_rows(q, place[h])],
                s4_send.at[q, h, k], s4_recv.at[q, h, k], along[h][k][0],
            )
            for k, h in pairs
        ]
        for q in range(PIECES)
    ]

    gathered = users[...].reshape(2 * DEPTH * SHARE, PANEL)
    for q in range(PIECES):
        rows = pl.ds(q * piece, piece)
        below = jnp.dot(turned[rows, :], gathered, preferred_element_type=jnp.float32)
        for h in range(2):
            part[h, rows, :] = below[:, h * BLOCK : (h + 1) * BLOCK]
        start(s1[q])

    def diag_rows(device_user):
        return pl.ds(pl.multiple_of((core * SIDE * SIDE + device_user) * TILE, TILE), TILE)

    diag[...] = lax.dot_general(
        gathered, gathered, (((0,), (0,)), ((), ())), preferred_element_type=jnp.float32
    )
    ds_copies = [
        remote(diag.at[diag_rows(d[0])], diag_in.at[user], ds_send.at[k], ds_recv.at[k], d)
        for k, d in enumerate(xy_ids)
    ]
    start(ds_copies)
    diag_in[user] = diag[diag_rows(user), :]
    wait(ds_copies)
    diag_sum = diag_in[0]
    for k in range(1, SIDE * SIDE):
        diag_sum = diag_sum + diag_in[k]
    row = lax.broadcasted_iota(jnp.int32, (TILE, PANEL), 0) + (core * SIDE * SIDE + user) * TILE
    col = lax.broadcasted_iota(jnp.int32, (TILE, PANEL), 1)
    work[diag_rows(user), :] = diag_sum + jnp.where(row == col, 0.5, 0.0)
    dg_copies = [
        remote(work.at[diag_rows(user)], work.at[diag_rows(user)], dg_send.at[k], dg_recv.at[k], d)
        for k, d in enumerate(xy_ids)
    ]
    start(dg_copies)
    core_half = pl.ds(pl.multiple_of(core * BLOCK, BLOCK), BLOCK)
    half_copy = remote(work.at[core_half], work.at[core_half], half_sem.at[0], half_sem.at[1], core_id)

    for q in range(PIECES):
        wait(s1[q])
        for h in range(2):
            sum1[q, h] = part[h, big_rows(q, place[h]), :] + in1[q, h, 0] + in1[q, h, 1] + in1[q, h, 2]
        start(s2[q])

    for what, n in ORDER:
        if what == "diag":
            wait(dg_copies)
            half_copy.start()
            half_copy.wait()
        elif what == "factor":
            factor_step(n, work, upper_ref)
        elif what == "sum":
            wait(s2[n])
            for h in range(2):
                mine = sum1[n, h, pl.ds(pl.multiple_of(place[1 - h] * small, small), small), :]
                total[h, own_rows(n, h), :] = mine + in2[n, h, 0] + in2[n, h, 1] + in2[n, h, 2]
            start(s3[n])
        else:
            wait(s3[n])
            start(s4[n])
    upper_ref[...] = upper_ref[...].T
    stores = [pltpu.make_async_copy(upper_ref, diag_out, store_sem.at[PIECES])]
    start(stores)

    for q in range(PIECES):
        wait(s4[q])
        rows = pl.ds(q * piece, piece)
        below_ref[rows, :] = lax.dot_general(
            jnp.concatenate([total[0, rows, :], total[1, rows, :]], 1), work[...], (((1,), (1,)), ((), ())),
            precision=lax.Precision.HIGHEST, preferred_element_type=jnp.float32,
        )
        stores.append(pltpu.make_async_copy(below_ref.at[rows], below_out.at[rows], store_sem.at[q]))
        stores[-1].start()
    wait(stores)


def store_kernel(diag_ref, below_ref, diag_out, below_out):
    diag_out[...] = diag_ref[...]
    below_out[...] = below_ref[...]


def on_device(panel_users, block_values, block_list, block_count):
    f32, bf16 = jnp.float32, jnp.bfloat16
    slots = block_values.shape[1]
    values = block_values.transpose(1, 0, 2).reshape(slots, DEPTH, 2, SHARE, BLOCK)
    vmem = pl.BlockSpec(memory_space=pltpu.VMEM)
    hbm = pl.BlockSpec(memory_space=pltpu.HBM)
    sems = pltpu.SemaphoreType.DMA
    xy = SIDE * SIDE - 1
    big, small = ROWS // PIECES // SIDE, ROWS // PIECES // SIDE**2
    out_shape = [jax.ShapeDtypeStruct((PANEL, PANEL), f32), jax.ShapeDtypeStruct((ROWS, PANEL), f32)]
    diag, below = pl.pallas_call(
        gram_kernel,
        out_shape=out_shape,
        in_specs=[hbm, hbm, hbm, hbm],
        out_specs=[hbm, hbm],
        scratch_shapes=[
            pltpu.VMEM((2, DEPTH, SHARE, PANEL), bf16),
            pltpu.VMEM((2, BLK_DEV, DEPTH, SHARE, BLOCK), bf16),
            pltpu.VMEM((ROWS, 2 * DEPTH * SHARE), bf16),
            pltpu.SMEM((1, slots), jnp.int32),
            pltpu.SMEM((1, 1), jnp.int32),
            pltpu.VMEM((PANEL, PANEL), f32),
            pltpu.VMEM((SIDE * SIDE, TILE, PANEL), f32),
            pltpu.VMEM((PANEL, PANEL), f32),
            pltpu.VMEM((2, ROWS, BLOCK), f32),
            pltpu.VMEM((PIECES, 2, SIDE - 1, big, BLOCK), f32),
            pltpu.VMEM((PIECES, 2, big, BLOCK), f32),
            pltpu.VMEM((PIECES, 2, SIDE - 1, small, BLOCK), f32),
            pltpu.VMEM((2, ROWS, BLOCK), f32),
            pltpu.VMEM((PANEL, PANEL), f32),
            pltpu.VMEM((ROWS, PANEL), f32),
            sems((5,)),
            sems((PIECES + 1,)),
            sems((DEPTH - 1,)),
            sems((DEPTH - 1,)),
            sems((DEPTH,)),
            sems((DEPTH,)),
            sems((xy,)),
            sems((xy,)),
            sems((xy,)),
            sems((xy,)),
            sems((2,)),
        ]
        + [sems((PIECES, 2, SIDE - 1))] * 8,
        compiler_params=pltpu.CompilerParams(
            collective_id=0, has_side_effects=True, vmem_limit_bytes=56 << 20
        ),
        name="gram",
    )(panel_users, values, block_list, block_count)
    whole = pl.BlockSpec((PANEL, PANEL), lambda i: (0, 0))
    rows = pl.BlockSpec((ROWS // STORES, PANEL), lambda i: (i, 0))
    return pl.pallas_call(
        store_kernel,
        grid=(STORES,),
        out_shape=out_shape,
        in_specs=[whole, rows],
        out_specs=[whole, rows],
        compiler_params=pltpu.CompilerParams(vmem_limit_bytes=56 << 20),
        name="store",
    )(diag, below)


def solution(mesh):
    in_specs = (
        P(("user", "item"), None),
        P("user", "item", None),
        P("user", "item"),
        P("user", "item"),
    )
    out_specs = (P(), P("item", None))
    return jax.shard_map(
        on_device, mesh=mesh, in_specs=in_specs, out_specs=out_specs, check_vma=False
    )
```

time: 237 us -> 63.1 us (0.27)
  waiting for transfers between devices: 113 us -> 0 us
  Pallas kernels: 0 us -> 61.6 us
  other arithmetic: 55.6 us -> 0 us
  blocking collectives: 38.7 us -> 0 us
  between operations: 16.1 us -> 1.28 us
  local copies, waits for them, and re-layouts: 8.23 us -> 0 us
  matrix products: 5.2 us -> 0 us
    psum x1 -> x0, waiting for transfers between devices: 113 us -> none  [on_device(): diag_total, below_total = lax.psum((diag_part, below_part), 'user')]
    pallas_call x0 -> x2, Pallas kernels: none -> 61.6 us  [the longest x1 58 us: on_device(): pl.pallas_call(gram_kernel, out_shape=out_shape, in_specs=[hbm, hbm, hbm,...]
    another operation x10 -> x0, other arithmetic: 54.6 us -> none  [the longest x6 34.1 us: on_device(): factor_diag = jnp.linalg.cholesky(diag_total + identity)]
    all_gather x1 -> x0, blocking collectives: 38.7 us -> none  [on_device(): gathered = lax.all_gather(panel_users, 'item', axis=0, tiled=True)]
    another operation x9 -> x0, local copies, waits for them, and re-layouts: 4.02 us -> none
    unnamed x9 -> x0, local copies, waits for them, and re-layouts: 2.78 us -> none
    another operation x5 -> x0, matrix products: 2.7 us -> none  [the longest x3 2.23 us: solve_rows(): lax.linalg.triangular_solve(factor_diag, rows, left_side=False, lower=Tru...]
    dot_general x3 -> x0, matrix products: 2.5 us -> none  [the longest x1 1.09 us: on_device(): jnp.einsum('kb,kcp->bcp', chosen.astype(jnp.float32), product, precision=...]
  transfers between devices with their start and end apart: 1 -> 0, of which waited for: 1 -> 0; matrix products, arithmetic and copies ran while one was open for 0% -> 0% of each run, Pallas kernels for 0% -> 0%
where the time goes in v2:
time: 63.1 us; the launch traced here: 62.9 us
  Pallas kernels  61.6 us (98%)
  between operations  1.28 us (2%)
    pallas_call x1, Pallas kernels, on_device(): pl.pallas_call(gram_kernel, out_shape=out_shape, in_specs=[hbm, hbm, hbm,...  58 us
    pallas_call x1, Pallas kernels, on_device(): pl.pallas_call(store_kernel, grid=(STORES,), out_shape=out_shape, in_spec...  3.57 us

profile of v2, /device:TPU:1, one launch (start us, length us, event | category | flops | bytes accessed | tf_op | source)
XLA Modules:
  0.0 62.9 jit_solution(16904290308189029959)
XLA Ops:
  1.3 58.0 %gram.1 = (f32[256,256]{1,0:T(8,128)}, f32[1024,256]{1,0:T(8,128)}) custom-call(bf16[16,256]{1,0:T(8,128)(2,1)} %panel_ref.1, bf16[7,16,2,16,128]{4,3,2,1,0:T(8,128)(2,1)} %bitcast.3, s32[1,7]{1,0:T(1,128)} %list_ref.1, s32[1,1]{1,0:T(1,128)S(6)} %copy.6.count_ref), custom_call_target="tpu_custom_call" | custom-call | tf_op jit(solution)/shard_map/gram/pallas_call | solution.py:324
  59.3 3.6 %store.1 = (f32[256,256]{1,0:T(8,128)}, f32[1024,256]{1,0:T(8,128)}) custom-call(f32[256,256]{1,0:T(8,128)} %get-tuple-element.4.diag_ref, f32[1024,256]{1,0:T(8,128)} %get-tuple-element.5.below_ref), custom_call_target="tpu_custom_call" | custom-call | tf_op jit(solution)/shard_map/store/pallas_call | solution.py:365

commit v3 on v2

--- a/solution.py
+++ b/solution.py
@@ -24,8 +24,9 @@
 )
 FAR_FIRST_SIDE = (2, 1, 3)
 ORDER = (
-    ("sum", 0), ("sum", 1), ("diag", 0), ("factor", 0), ("sum", 2), ("factor", 1), ("sum", 3), ("pass", 0), ("factor", 2),
-    ("pass", 1), ("factor", 3), ("pass", 2), ("factor", 4), ("pass", 3), ("factor", 5), ("factor", 6), ("factor", 7),
+    ("sum", 0), ("sum", 1), ("half", 0), ("sum", 2), ("diag", 0), ("factor", 0), ("sum", 3), ("pass", 0), ("factor", 1),
+    ("pass", 1), ("factor", 2), ("pass", 2), ("factor", 3), ("pass", 3), ("factor", 4), ("factor", 5), ("factor", 6),
+    ("factor", 7),
 )
 
 
@@ -95,9 +96,9 @@
 
 
 def gram_kernel(
-    panel_ref, values_ref, list_ref, count_ref, diag_out, below_out,
-    users, values, turned, slot_list, slot_count, diag, diag_in, work, part, in1, sum1, in2, total, upper_ref, below_ref,
-    load_sem, store_sem, z_send, z_recv, core_send, core_recv, ds_send, ds_recv, dg_send, dg_recv, half_sem,
+    panel_ref, values_ref, list_ref, count_ref, upper_ref, work, total,
+    users, values, turned, slot_list, diag, diag_in, part, in1, sum1, in2,
+    load_sem, z_send, z_recv, core_send, core_recv, ds_send, ds_recv, dg_send, dg_recv, half_sem,
     s1_send, s1_recv, s2_send, s2_recv, s3_send, s3_recv, s4_send, s4_recv,
 ):
     user = lax.axis_index("user")
@@ -131,11 +132,8 @@
         pl.semaphore_signal(barrier, inc=1, device_id=device, device_id_type=MESH)
 
     own_load = pltpu.make_async_copy(panel_ref, users.at[core, z], load_sem.at[0])
-    loads = [
-        pltpu.make_async_copy(list_ref, slot_list, load_sem.at[1]),
-        pltpu.make_async_copy(count_ref, slot_count, load_sem.at[2]),
-    ] + [
-        pltpu.make_async_copy(values_ref.at[:, :, c], values.at[c, pl.ds(0, BLK_DEV - 1)], load_sem.at[3 + c])
+    loads = [pltpu.make_async_copy(list_ref, slot_list, load_sem.at[1])] + [
+        pltpu.make_async_copy(values_ref.at[:, :, c], values.at[c, pl.ds(0, BLK_DEV - 1)], load_sem.at[2 + c])
         for c in range(2)
     ]
     start([own_load] + loads)
@@ -158,7 +156,7 @@
     core_copies[0].start()
 
     wait(loads)
-    used = slot_count[0, 0]
+    used = count_ref[0, 0]
     for b in range(BLK_DEV):
         slot = jnp.int32(BLK_DEV - 1)
         for k in range(BLK_DEV - 1):
@@ -234,6 +232,18 @@
     ]
 
     gathered = users[...].reshape(2 * DEPTH * SHARE, PANEL)
+    def diag_rows(device_user):
+        return pl.ds(pl.multiple_of((core * SIDE * SIDE + device_user) * TILE, TILE), TILE)
+
+    diag[...] = lax.dot_general(
+        gathered, gathered, (((0,), (0,)), ((), ())), preferred_element_type=jnp.float32
+    )
+    ds_copies = [
+        remote(diag.at[diag_rows(d[0])], diag_in.at[user], ds_send.at[k], ds_recv.at[k], d)
+        for k, d in enumerate(xy_ids)
+    ]
+    start(ds_copies)
+    diag_in[user] = diag[diag_rows(user), :]
     for q in range(PIECES):
         rows = pl.ds(q * piece, piece)
         below = jnp.dot(turned[rows, :], gathered, preferred_element_type=jnp.float32)
@@ -241,18 +251,6 @@
             part[h, rows, :] = below[:, h * BLOCK : (h + 1) * BLOCK]
         start(s1[q])
 
-    def diag_rows(device_user):
-        return pl.ds(pl.multiple_of((core * SIDE * SIDE + device_user) * TILE, TILE), TILE)
-
-    diag[...] = lax.dot_general(
-        gathered, gathered, (((0,), (0,)), ((), ())), preferred_element_type=jnp.float32
-    )
-    ds_copies = [
-        remote(diag.at[diag_rows(d[0])], diag_in.at[user], ds_send.at[k], ds_recv.at[k], d)
-        for k, d in enumerate(xy_ids)
-    ]
-    start(ds_copies)
-    diag_in[user] = diag[diag_rows(user), :]
     wait(ds_copies)
     diag_sum = diag_in[0]
     for k in range(1, SIDE * SIDE):
@@ -275,9 +273,10 @@
         start(s2[q])
 
     for what, n in ORDER:
-        if what == "diag":
+        if what == "half":
             wait(dg_copies)
             half_copy.start()
+        elif what == "diag":
             half_copy.wait()
         elif what == "factor":
             factor_step(n, work, upper_ref)
@@ -290,25 +289,26 @@
         else:
             wait(s3[n])
             start(s4[n])
-    upper_ref[...] = upper_ref[...].T
-    stores = [pltpu.make_async_copy(upper_ref, diag_out, store_sem.at[PIECES])]
-    start(stores)
-
     for q in range(PIECES):
         wait(s4[q])
-        rows = pl.ds(q * piece, piece)
-        below_ref[rows, :] = lax.dot_general(
-            jnp.concatenate([total[0, rows, :], total[1, rows, :]], 1), work[...], (((1,), (1,)), ((), ())),
+
+
+def solve_kernel(upper_ref, inverse_ref, total_ref, diag_out, below_out, lower, below, sem):
+    stores = []
+    for i in range(STORES):
+        rows = pl.ds(i * (ROWS // STORES), ROWS // STORES)
+        below[rows, :] = lax.dot_general(
+            jnp.concatenate([total_ref[0, rows, :], total_ref[1, rows, :]], 1), inverse_ref[...],
+            (((1,), (1,)), ((), ())),
             precision=lax.Precision.HIGHEST, preferred_element_type=jnp.float32,
         )
-        stores.append(pltpu.make_async_copy(below_ref.at[rows], below_out.at[rows], store_sem.at[q]))
+        stores.append(pltpu.make_async_copy(below.at[rows], below_out.at[rows], sem.at[i]))
         stores[-1].start()
-    wait(stores)
-
-
-def store_kernel(diag_ref, below_ref, diag_out, below_out):
-    diag_out[...] = diag_ref[...]
-    below_out[...] = below_ref[...]
+    lower[...] = upper_ref[...].T
+    stores.append(pltpu.make_async_copy(lower, diag_out, sem.at[STORES]))
+    stores[-1].start()
+    for store in stores:
+        store.wait()
 
 
 def on_device(panel_users, block_values, block_list, block_count):
@@ -320,30 +320,27 @@
     sems = pltpu.SemaphoreType.DMA
     xy = SIDE * SIDE - 1
     big, small = ROWS // PIECES // SIDE, ROWS // PIECES // SIDE**2
-    out_shape = [jax.ShapeDtypeStruct((PANEL, PANEL), f32), jax.ShapeDtypeStruct((ROWS, PANEL), f32)]
-    diag, below = pl.pallas_call(
+    upper, inverse, total = pl.pallas_call(
         gram_kernel,
-        out_shape=out_shape,
-        in_specs=[hbm, hbm, hbm, hbm],
-        out_specs=[hbm, hbm],
+        out_shape=[
+            pltpu.VMEM((PANEL, PANEL), f32),
+            pltpu.VMEM((PANEL, PANEL), f32),
+            pltpu.VMEM((2, ROWS, BLOCK), f32),
+        ],
+        in_specs=[hbm, hbm, hbm, pl.BlockSpec(memory_space=pltpu.SMEM)],
+        out_specs=[vmem, vmem, vmem],
         scratch_shapes=[
             pltpu.VMEM((2, DEPTH, SHARE, PANEL), bf16),
             pltpu.VMEM((2, BLK_DEV, DEPTH, SHARE, BLOCK), bf16),
             pltpu.VMEM((ROWS, 2 * DEPTH * SHARE), bf16),
             pltpu.SMEM((1, slots), jnp.int32),
-            pltpu.SMEM((1, 1), jnp.int32),
             pltpu.VMEM((PANEL, PANEL), f32),
             pltpu.VMEM((SIDE * SIDE, TILE, PANEL), f32),
-            pltpu.VMEM((PANEL, PANEL), f32),
             pltpu.VMEM((2, ROWS, BLOCK), f32),
             pltpu.VMEM((PIECES, 2, SIDE - 1, big, BLOCK), f32),
             pltpu.VMEM((PIECES, 2, big, BLOCK), f32),
             pltpu.VMEM((PIECES, 2, SIDE - 1, small, BLOCK), f32),
-            pltpu.VMEM((2, ROWS, BLOCK), f32),
-            pltpu.VMEM((PANEL, PANEL), f32),
-            pltpu.VMEM((ROWS, PANEL), f32),
-            sems((5,)),
-            sems((PIECES + 1,)),
+            sems((4,)),
             sems((DEPTH - 1,)),
             sems((DEPTH - 1,)),
             sems((DEPTH,)),
@@ -356,21 +353,19 @@
         ]
         + [sems((PIECES, 2, SIDE - 1))] * 8,
         compiler_params=pltpu.CompilerParams(
-            collective_id=0, has_side_effects=True, vmem_limit_bytes=56 << 20
+            collective_id=0, has_side_effects=True, vmem_limit_bytes=32 << 20
         ),
         name="gram",
-    )(panel_users, values, block_list, block_count)
-    whole = pl.BlockSpec((PANEL, PANEL), lambda i: (0, 0))
-    rows = pl.BlockSpec((ROWS // STORES, PANEL), lambda i: (i, 0))
+    )(*[pltpu.with_memory_space_constraint(a, pltpu.HBM) for a in (panel_users, values, block_list)], block_count)
     return pl.pallas_call(
-        store_kernel,
-        grid=(STORES,),
-        out_shape=out_shape,
-        in_specs=[whole, rows],
-        out_specs=[whole, rows],
-        compiler_params=pltpu.CompilerParams(vmem_limit_bytes=56 << 20),
-        name="store",
-    )(diag, below)
+        solve_kernel,
+        out_shape=[jax.ShapeDtypeStruct((PANEL, PANEL), f32), jax.ShapeDtypeStruct((ROWS, PANEL), f32)],
+        in_specs=[vmem] * 3,
+        out_specs=[hbm] * 2,
+        scratch_shapes=[pltpu.VMEM((PANEL, PANEL), f32), pltpu.VMEM((ROWS, PANEL), f32), sems((STORES + 1,))],
+        compiler_params=pltpu.CompilerParams(vmem_limit_bytes=16 << 20),
+        name="solve",
+    )(upper, inverse, total)
 
 
 def solution(mesh):

time: 63.1 us -> 55.5 us (0.88)
  Pallas kernels: 61.6 us -> 54.1 us
    pallas_call x2, Pallas kernels: 61.6 us -> 54.1 us  [the longest x1 52.1 us: on_device(): pl.pallas_call(gram_kernel, out_shape=[pltpu.VMEM((PANEL, PANEL), f32), p...]
where the time goes in v3:
time: 55.5 us; the launch traced here: 55.3 us
  Pallas kernels  54.1 us (97%)
  between operations  1.28 us (2%)
    pallas_call x1, Pallas kernels, on_device(): pl.pallas_call(gram_kernel, out_shape=[pltpu.VMEM((PANEL, PANEL), f32), p...  52.1 us
    pallas_call x1, Pallas kernels, on_device(): pl.pallas_call(solve_kernel, out_shape=[jax.ShapeDtypeStruct((PANEL, PANE...  1.97 us

profile of v3, /device:TPU:1, one launch (start us, length us, event | category | flops | bytes accessed | tf_op | source)
XLA Modules:
  0.0 55.3 jit_solution(10497707419506773010)
XLA Ops:
  1.3 52.1 %gram.1 = (f32[256,256]{1,0:T(8,128)S(1)}, f32[256,256]{1,0:T(8,128)S(1)}, f32[2,1024,128]{2,1,0:T(8,128)S(1)}) custom-call(bf16[16,256]{1,0:T(8,128)(2,1)} %panel_ref.1, bf16[7,16,2,16,128]{4,3,2,1,0:T(8,128)(2,1)} %bitcast.3, s32[1,7]{1,0:T(1,128)} %list_ref.1, s32[1,1]{1,0:T(1,128)S(6)} %copy.6.count_ref), custom_call_target="tpu_custom_call" | custom-call | tf_op jit(solution)/shard_map/gram/pallas_call | solution.py:323
  53.4 2.0 %solve.1 = (f32[256,256]{1,0:T(8,128)}, f32[1024,256]{1,0:T(8,128)}) custom-call(f32[256,256]{1,0:T(8,128)S(1)} %get-tuple-element.5.upper_ref, f32[256,256]{1,0:T(8,128)S(1)} %get-tuple-element.6.inverse_ref, f32[2,1024,128]{2,1,0:T(8,128)S(1)} %get-tuple-element.7.total_ref), custom_call_target="tpu_custom_call" | custom-call | tf_op jit(solution)/shard_map/solve/pallas_call | solution.py:360

commit v4 on v3

--- a/solution.py
+++ b/solution.py
@@ -17,7 +17,8 @@
 STORES = 4
 PIECES = 4
 MESH = pl.DeviceIdType.MESH
-FAR_FIRST_Z = (8, 7, 9, 6, 10, 5, 11, 4, 12, 3, 13, 2, 14, 1, 15)
+REACH = 4
+NEAR_Z = (4, -4, 3, -3, 2, -2, 1, -1)
 FAR_FIRST_XY = sorted(
     ((dy, dx) for dy in range(SIDE) for dx in range(SIDE) if dy or dx),
     key=lambda d: -(min(d[0], SIDE - d[0]) + min(d[1], SIDE - d[1])),
@@ -98,7 +99,7 @@
 def gram_kernel(
     panel_ref, values_ref, list_ref, count_ref, upper_ref, work, total,
     users, values, turned, slot_list, diag, diag_in, part, in1, sum1, in2,
-    load_sem, z_send, z_recv, core_send, core_recv, ds_send, ds_recv, dg_send, dg_recv, half_sem,
+    load_sem, z_send, z_recv, f_send, f_recv, core_send, core_recv, ds_send, ds_recv, dg_send, dg_recv, half_sem,
     s1_send, s1_recv, s2_send, s2_recv, s3_send, s3_recv, s4_send, s4_recv,
 ):
     user = lax.axis_index("user")
@@ -110,7 +111,10 @@
     def at_xy(dy, dx):
         return ((y + dy) % SIDE) * SIDE + (x + dx) % SIDE
 
-    z_ids = [(user, ((z + d) % DEPTH) * 2 + core) for d in FAR_FIRST_Z]
+    def at_z(d):
+        return (z + DEPTH + d) % DEPTH
+
+    z_ids = [(user, at_z(d) * 2 + core) for d in NEAR_Z]
     xy_ids = [(at_xy(*d), item) for d in FAR_FIRST_XY]
     core_id = (user, z * 2 + other)
 
@@ -123,9 +127,8 @@
         for copy in copies:
             copy.start()
 
-    def wait(copies):
-        for copy in copies:
-            copy.wait()
+    def wait(ref, sem):
+        pltpu.make_async_copy(ref, ref, sem).wait()
 
     barrier = pltpu.get_barrier_semaphore()
     for device in z_ids + xy_ids + [core_id]:
@@ -143,19 +146,18 @@
     pl.semaphore_wait(barrier, len(z_ids) + len(xy_ids) + 1)
 
     z_copies = [
-        remote(users.at[core, z], users.at[core, z], z_send.at[k], z_recv.at[k], device)
+        remote(users.at[core, z], users.at[core, z], z_send, z_recv.at[k], device)
         for k, device in enumerate(z_ids)
     ]
     start(z_copies)
-    core_copies = []
-    for k, d in enumerate((0,) + FAR_FIRST_Z):
-        came_from = (z + DEPTH - d) % DEPTH
-        core_copies.append(
-            remote(users.at[core, came_from], users.at[core, came_from], core_send.at[k], core_recv.at[k], core_id)
-        )
-    core_copies[0].start()
-
-    wait(loads)
+
+    def pass_to_core(place):
+        return remote(users.at[core, place], users.at[core, place], core_send, core_recv, core_id)
+
+    pass_to_core(z).start()
+
+    for load in loads:
+        load.wait()
     used = count_ref[0, 0]
     for b in range(BLK_DEV):
         slot = jnp.int32(BLK_DEV - 1)
@@ -165,12 +167,24 @@
             block = values[c, slot].reshape(DEPTH * SHARE, BLOCK)
             turned[pl.ds(b * BLOCK, BLOCK), pl.ds(c * DEPTH * SHARE, DEPTH * SHARE)] = block.T
 
-    for k in reversed(range(DEPTH - 1)):
+    passed = []
+    for k, d in reversed(list(enumerate(NEAR_Z))):
         z_copies[k].wait_recv()
-        core_copies[k + 1].start()
-    wait(core_copies)
-    for copy in z_copies:
-        copy.wait_send()
+        came_from = at_z(-d)
+        if d != -REACH:
+            ahead = (user, at_z(REACH if d > 0 else -REACH) * 2 + core)
+            f = len(passed)
+            copy = remote(users.at[core, came_from], users.at[core, came_from], f_send, f_recv.at[f], ahead)
+            copy.start()
+            passed.append((copy, at_z(-d - (REACH if d > 0 else -REACH))))
+        pass_to_core(came_from).start()
+    for copy, came_from in passed:
+        copy.wait_recv()
+        pass_to_core(came_from).start()
+    wait(users.at[other], core_recv)
+    wait(users.at[core], core_send)
+    wait(users.at[core, pl.ds(0, len(z_copies))], z_send)
+    wait(users.at[core, pl.ds(0, len(passed))], f_send)
 
     along = (
         [((at_xy(0, d), item), (x + d) % SIDE) for d in FAR_FIRST_SIDE],
@@ -194,7 +208,7 @@
         [
             remote(
                 part.at[h, big_rows(q, along[h][k][1])], in1.at[q, h, k],
-                s1_send.at[q, h, k], s1_recv.at[q, h, k], along[h][k][0],
+                s1_send, s1_recv.at[q], along[h][k][0],
             )
             for k, h in pairs
         ]
@@ -204,7 +218,7 @@
         [
             remote(
                 sum1.at[q, h, pl.ds(pl.multiple_of(along[1 - h][k][1] * small, small), small)], in2.at[q, h, k],
-                s2_send.at[q, h, k], s2_recv.at[q, h, k], along[1 - h][k][0],
+                s2_send, s2_recv.at[q], along[1 - h][k][0],
             )
             for k, h in pairs
         ]
@@ -214,7 +228,7 @@
         [
             remote(
                 total.at[h, own_rows(q, h)], total.at[h, own_rows(q, h)],
-                s3_send.at[q, h, k], s3_recv.at[q, h, k], along[1 - h][k][0],
+                s3_send, s3_recv.at[q], along[1 - h][k][0],
             )
             for k, h in pairs
         ]
@@ -224,7 +238,7 @@
         [
             remote(
                 total.at[h, big_rows(q, place[h])], total.at[h, big_rows(q, place[h])],
-                s4_send.at[q, h, k], s4_recv.at[q, h, k], along[h][k][0],
+                s4_send, s4_recv.at[q], along[h][k][0],
             )
             for k, h in pairs
         ]
@@ -239,8 +253,8 @@
         gathered, gathered, (((0,), (0,)), ((), ())), preferred_element_type=jnp.float32
     )
     ds_copies = [
-        remote(diag.at[diag_rows(d[0])], diag_in.at[user], ds_send.at[k], ds_recv.at[k], d)
-        for k, d in enumerate(xy_ids)
+        remote(diag.at[diag_rows(d[0])], diag_in.at[user], ds_send, ds_recv, d)
+        for d in xy_ids
     ]
     start(ds_copies)
     diag_in[user] = diag[diag_rows(user), :]
@@ -251,7 +265,8 @@
             part[h, rows, :] = below[:, h * BLOCK : (h + 1) * BLOCK]
         start(s1[q])
 
-    wait(ds_copies)
+    others = diag_in.at[pl.ds(0, len(xy_ids))]
+    wait(others, ds_recv)
     diag_sum = diag_in[0]
     for k in range(1, SIDE * SIDE):
         diag_sum = diag_sum + diag_in[k]
@@ -259,38 +274,44 @@
     col = lax.broadcasted_iota(jnp.int32, (TILE, PANEL), 1)
     work[diag_rows(user), :] = diag_sum + jnp.where(row == col, 0.5, 0.0)
     dg_copies = [
-        remote(work.at[diag_rows(user)], work.at[diag_rows(user)], dg_send.at[k], dg_recv.at[k], d)
-        for k, d in enumerate(xy_ids)
+        remote(work.at[diag_rows(user)], work.at[diag_rows(user)], dg_send, dg_recv, d)
+        for d in xy_ids
     ]
     start(dg_copies)
     core_half = pl.ds(pl.multiple_of(core * BLOCK, BLOCK), BLOCK)
     half_copy = remote(work.at[core_half], work.at[core_half], half_sem.at[0], half_sem.at[1], core_id)
 
     for q in range(PIECES):
-        wait(s1[q])
+        wait(in1.at[q], s1_recv.at[q])
         for h in range(2):
             sum1[q, h] = part[h, big_rows(q, place[h]), :] + in1[q, h, 0] + in1[q, h, 1] + in1[q, h, 2]
         start(s2[q])
 
     for what, n in ORDER:
         if what == "half":
-            wait(dg_copies)
+            wait(others, dg_recv)
+            wait(others, dg_send)
             half_copy.start()
         elif what == "diag":
             half_copy.wait()
         elif what == "factor":
             factor_step(n, work, upper_ref)
         elif what == "sum":
-            wait(s2[n])
+            wait(in2.at[n], s2_recv.at[n])
             for h in range(2):
                 mine = sum1[n, h, pl.ds(pl.multiple_of(place[1 - h] * small, small), small), :]
                 total[h, own_rows(n, h), :] = mine + in2[n, h, 0] + in2[n, h, 1] + in2[n, h, 2]
             start(s3[n])
         else:
-            wait(s3[n])
+            wait(in2.at[n], s3_recv.at[n])
             start(s4[n])
     for q in range(PIECES):
-        wait(s4[q])
+        wait(in1.at[q], s4_recv.at[q])
+    wait(in1, s1_send)
+    wait(in2, s2_send)
+    wait(in2, s3_send)
+    wait(in1, s4_send)
+    wait(others, ds_send)
 
 
 def solve_kernel(upper_ref, inverse_ref, total_ref, diag_out, below_out, lower, below, sem):
@@ -318,7 +339,6 @@
     vmem = pl.BlockSpec(memory_space=pltpu.VMEM)
     hbm = pl.BlockSpec(memory_space=pltpu.HBM)
     sems = pltpu.SemaphoreType.DMA
-    xy = SIDE * SIDE - 1
     big, small = ROWS // PIECES // SIDE, ROWS // PIECES // SIDE**2
     upper, inverse, total = pl.pallas_call(
         gram_kernel,
@@ -341,17 +361,14 @@
             pltpu.VMEM((PIECES, 2, big, BLOCK), f32),
             pltpu.VMEM((PIECES, 2, SIDE - 1, small, BLOCK), f32),
             sems((4,)),
-            sems((DEPTH - 1,)),
-            sems((DEPTH - 1,)),
-            sems((DEPTH,)),
-            sems((DEPTH,)),
-            sems((xy,)),
-            sems((xy,)),
-            sems((xy,)),
-            sems((xy,)),
-            sems((2,)),
-        ]
-        + [sems((PIECES, 2, SIDE - 1))] * 8,
+            sems,
+            sems((2 * REACH,)),
+            sems,
+            sems((2 * REACH - 1,)),
+        ]
+        + [sems] * 6
+        + [sems((2,))]
+        + [sems, sems((PIECES,))] * 4,
         compiler_params=pltpu.CompilerParams(
             collective_id=0, has_side_effects=True, vmem_limit_bytes=32 << 20
         ),

time: 55.5 us -> 53 us (0.955)
  Pallas kernels: 54.1 us -> 51.6 us
    pallas_call x1, Pallas kernels: 52.1 us -> 49.6 us  [on_device(): pl.pallas_call(gram_kernel, out_shape=[pltpu.VMEM((PANEL, PANEL), f32), p...]
where the time goes in v4:
time: 53 us; the launch traced here: 52.9 us
  Pallas kernels  51.6 us (97%)
  between operations  1.28 us (2%)
    pallas_call x1, Pallas kernels, on_device(): pl.pallas_call(gram_kernel, out_shape=[pltpu.VMEM((PANEL, PANEL), f32), p...  49.6 us
    pallas_call x1, Pallas kernels, on_device(): pl.pallas_call(solve_kernel, out_shape=[jax.ShapeDtypeStruct((PANEL, PANE...  1.97 us

profile of v4, /device:TPU:1, one launch (start us, length us, event | category | flops | bytes accessed | tf_op | source)
XLA Modules:
  0.0 52.9 jit_solution(14884186122256391293)
XLA Ops:
  1.3 49.6 %gram.1 = (f32[256,256]{1,0:T(8,128)S(1)}, f32[256,256]{1,0:T(8,128)S(1)}, f32[2,1024,128]{2,1,0:T(8,128)S(1)}) custom-call(bf16[16,256]{1,0:T(8,128)(2,1)} %panel_ref.1, bf16[7,16,2,16,128]{4,3,2,1,0:T(8,128)(2,1)} %bitcast.3, s32[1,7]{1,0:T(1,128)} %list_ref.1, s32[1,1]{1,0:T(1,128)S(6)} %copy.6.count_ref), custom_call_target="tpu_custom_call" | custom-call | tf_op jit(solution)/shard_map/gram/pallas_call | solution.py:343
  50.9 2.0 %solve.1 = (f32[256,256]{1,0:T(8,128)}, f32[1024,256]{1,0:T(8,128)}) custom-call(f32[256,256]{1,0:T(8,128)S(1)} %get-tuple-element.5.upper_ref, f32[256,256]{1,0:T(8,128)S(1)} %get-tuple-element.6.inverse_ref, f32[2,1024,128]{2,1,0:T(8,128)S(1)} %get-tuple-element.7.total_ref), custom_call_target="tpu_custom_call" | custom-call | tf_op jit(solution)/shard_map/solve/pallas_call | solution.py:377

commit v5 on v4

--- a/solution.py
+++ b/solution.py
@@ -134,27 +134,35 @@
     for device in z_ids + xy_ids + [core_id]:
         pl.semaphore_signal(barrier, inc=1, device_id=device, device_id_type=MESH)
 
-    own_load = pltpu.make_async_copy(panel_ref, users.at[core, z], load_sem.at[0])
-    loads = [pltpu.make_async_copy(list_ref, slot_list, load_sem.at[1])] + [
-        pltpu.make_async_copy(values_ref.at[:, :, c], values.at[c, pl.ds(0, BLK_DEV - 1)], load_sem.at[2 + c])
+    own_loads = [
+        pltpu.make_async_copy(panel_ref.at[:, pl.ds(p * BLOCK, BLOCK)], users.at[p, core, z], load_sem.at[p])
+        for p in range(2)
+    ]
+    loads = [pltpu.make_async_copy(list_ref, slot_list, load_sem.at[2])] + [
+        pltpu.make_async_copy(values_ref.at[:, :, c], values.at[c, pl.ds(0, BLK_DEV - 1)], load_sem.at[3 + c])
         for c in range(2)
     ]
-    start([own_load] + loads)
+    start(own_loads + loads)
     for c in range(2):
         values[c, BLK_DEV - 1] = jnp.zeros((DEPTH, SHARE, BLOCK), jnp.bfloat16)
-    own_load.wait()
+    for load in own_loads:
+        load.wait()
     pl.semaphore_wait(barrier, len(z_ids) + len(xy_ids) + 1)
 
     z_copies = [
-        remote(users.at[core, z], users.at[core, z], z_send, z_recv.at[k], device)
-        for k, device in enumerate(z_ids)
-    ]
-    start(z_copies)
-
-    def pass_to_core(place):
-        return remote(users.at[core, place], users.at[core, place], core_send, core_recv, core_id)
-
-    pass_to_core(z).start()
+        [
+            remote(users.at[p, core, z], users.at[p, core, z], z_send, z_recv.at[p, k], device)
+            for k, device in enumerate(z_ids)
+        ]
+        for p in range(2)
+    ]
+    start(z_copies[0] + z_copies[1])
+
+    def pass_to_core(p, place):
+        return remote(users.at[p, core, place], users.at[p, core, place], core_send, core_recv.at[p], core_id)
+
+    for p in range(2):
+        pass_to_core(p, z).start()
 
     for load in loads:
         load.wait()
@@ -167,24 +175,26 @@
             block = values[c, slot].reshape(DEPTH * SHARE, BLOCK)
             turned[pl.ds(b * BLOCK, BLOCK), pl.ds(c * DEPTH * SHARE, DEPTH * SHARE)] = block.T
 
-    passed = []
-    for k, d in reversed(list(enumerate(NEAR_Z))):
-        z_copies[k].wait_recv()
-        came_from = at_z(-d)
-        if d != -REACH:
-            ahead = (user, at_z(REACH if d > 0 else -REACH) * 2 + core)
-            f = len(passed)
-            copy = remote(users.at[core, came_from], users.at[core, came_from], f_send, f_recv.at[f], ahead)
-            copy.start()
-            passed.append((copy, at_z(-d - (REACH if d > 0 else -REACH))))
-        pass_to_core(came_from).start()
-    for copy, came_from in passed:
-        copy.wait_recv()
-        pass_to_core(came_from).start()
-    wait(users.at[other], core_recv)
-    wait(users.at[core], core_send)
-    wait(users.at[core, pl.ds(0, len(z_copies))], z_send)
-    wait(users.at[core, pl.ds(0, len(passed))], f_send)
+    passed = ([], [])
+    for p in range(2):
+        for k, d in reversed(list(enumerate(NEAR_Z))):
+            z_copies[p][k].wait_recv()
+            came_from = at_z(-d)
+            if d != -REACH:
+                way = REACH if d > 0 else -REACH
+                f = len(passed[p])
+                piece_ref = users.at[p, core, came_from]
+                copy = remote(piece_ref, piece_ref, f_send, f_recv.at[p, f], (user, at_z(way) * 2 + core))
+                copy.start()
+                passed[p].append((copy, at_z(-d - way)))
+            pass_to_core(p, came_from).start()
+
+    def finish_gather(p):
+        for copy, came_from in passed[p]:
+            copy.wait_recv()
+            pass_to_core(p, came_from).start()
+        wait(users.at[p, other], core_recv.at[p])
+        return users[p].reshape(2 * DEPTH * SHARE, BLOCK)
 
     along = (
         [((at_xy(0, d), item), (x + d) % SIDE) for d in FAR_FIRST_SIDE],
@@ -194,20 +204,26 @@
     piece = ROWS // PIECES
     big, small = piece // SIDE, piece // SIDE**2
 
-    def big_rows(q, i):
-        return pl.ds(pl.multiple_of(q * piece + i * big, big), big)
-
-    def small_rows(q, i):
-        return pl.ds(pl.multiple_of(q * piece + i * small, small), small)
+    def half_of(q):
+        return 2 * q // PIECES
+
+    def first_row(q, h):
+        return h * (ROWS // 2) + (q % (PIECES // 2)) * piece
+
+    def big_rows(q, h, i):
+        return pl.ds(pl.multiple_of(first_row(q, h) + i * big, big), big)
+
+    def small_rows(q, h, i):
+        return pl.ds(pl.multiple_of(first_row(q, h) + i * small, small), small)
 
     def own_rows(q, h):
-        return small_rows(q, place[h] * SIDE + place[1 - h])
+        return small_rows(q, h, place[h] * SIDE + place[1 - h])
 
     pairs = [(k, h) for k in range(SIDE - 1) for h in range(2)]
     s1 = [
         [
             remote(
-                part.at[h, big_rows(q, along[h][k][1])], in1.at[q, h, k],
+                part.at[half_of(q), big_rows(q, h, along[h][k][1])], in1.at[q, h, k],
                 s1_send, s1_recv.at[q], along[h][k][0],
             )
             for k, h in pairs
@@ -227,7 +243,7 @@
     s3 = [
         [
             remote(
-                total.at[h, own_rows(q, h)], total.at[h, own_rows(q, h)],
+                total.at[half_of(q), own_rows(q, h)], total.at[half_of(q), own_rows(q, h)],
                 s3_send, s3_recv.at[q], along[1 - h][k][0],
             )
             for k, h in pairs
@@ -237,7 +253,7 @@
     s4 = [
         [
             remote(
-                total.at[h, big_rows(q, place[h])], total.at[h, big_rows(q, place[h])],
+                total.at[half_of(q), big_rows(q, h, place[h])], total.at[half_of(q), big_rows(q, h, place[h])],
                 s4_send, s4_recv.at[q], along[h][k][0],
             )
             for k, h in pairs
@@ -245,25 +261,28 @@
         for q in range(PIECES)
     ]
 
-    gathered = users[...].reshape(2 * DEPTH * SHARE, PANEL)
+    def products(p, gathered):
+        for q in range(p * PIECES // 2, (p + 1) * PIECES // 2):
+            for h in range(2):
+                rows = pl.ds(first_row(q, h), piece)
+                part[p, rows, :] = jnp.dot(turned[rows, :], gathered, preferred_element_type=jnp.float32)
+            start(s1[q])
+
+    gathered0 = finish_gather(0)
+    products(0, gathered0)
+    gathered1 = finish_gather(1)
+
     def diag_rows(device_user):
         return pl.ds(pl.multiple_of((core * SIDE * SIDE + device_user) * TILE, TILE), TILE)
 
+    gathered = jnp.concatenate([gathered0, gathered1], 1)
     diag[...] = lax.dot_general(
         gathered, gathered, (((0,), (0,)), ((), ())), preferred_element_type=jnp.float32
     )
-    ds_copies = [
-        remote(diag.at[diag_rows(d[0])], diag_in.at[user], ds_send, ds_recv, d)
-        for d in xy_ids
-    ]
+    ds_copies = [remote(diag.at[diag_rows(d[0])], diag_in.at[user], ds_send, ds_recv, d) for d in xy_ids]
     start(ds_copies)
     diag_in[user] = diag[diag_rows(user), :]
-    for q in range(PIECES):
-        rows = pl.ds(q * piece, piece)
-        below = jnp.dot(turned[rows, :], gathered, preferred_element_type=jnp.float32)
-        for h in range(2):
-            part[h, rows, :] = below[:, h * BLOCK : (h + 1) * BLOCK]
-        start(s1[q])
+    products(1, gathered1)
 
     others = diag_in.at[pl.ds(0, len(xy_ids))]
     wait(others, ds_recv)
@@ -284,7 +303,7 @@
     for q in range(PIECES):
         wait(in1.at[q], s1_recv.at[q])
         for h in range(2):
-            sum1[q, h] = part[h, big_rows(q, place[h]), :] + in1[q, h, 0] + in1[q, h, 1] + in1[q, h, 2]
+            sum1[q, h] = part[half_of(q), big_rows(q, h, place[h]), :] + in1[q, h, 0] + in1[q, h, 1] + in1[q, h, 2]
         start(s2[q])
 
     for what, n in ORDER:
@@ -300,7 +319,7 @@
             wait(in2.at[n], s2_recv.at[n])
             for h in range(2):
                 mine = sum1[n, h, pl.ds(pl.multiple_of(place[1 - h] * small, small), small), :]
-                total[h, own_rows(n, h), :] = mine + in2[n, h, 0] + in2[n, h, 1] + in2[n, h, 2]
+                total[half_of(n), own_rows(n, h), :] = mine + in2[n, h, 0] + in2[n, h, 1] + in2[n, h, 2]
             start(s3[n])
         else:
             wait(in2.at[n], s3_recv.at[n])
@@ -312,6 +331,9 @@
     wait(in2, s3_send)
     wait(in1, s4_send)
     wait(others, ds_send)
+    wait(users.at[:, core], core_send)
+    wait(users.at[:, core, pl.ds(0, 2 * REACH)], z_send)
+    wait(users.at[:, core, pl.ds(0, 2 * REACH - 1)], f_send)
 
 
 def solve_kernel(upper_ref, inverse_ref, total_ref, diag_out, below_out, lower, below, sem):
@@ -350,7 +372,7 @@
         in_specs=[hbm, hbm, hbm, pl.BlockSpec(memory_space=pltpu.SMEM)],
         out_specs=[vmem, vmem, vmem],
         scratch_shapes=[
-            pltpu.VMEM((2, DEPTH, SHARE, PANEL), bf16),
+            pltpu.VMEM((2, 2, DEPTH, SHARE, BLOCK), bf16),
             pltpu.VMEM((2, BLK_DEV, DEPTH, SHARE, BLOCK), bf16),
             pltpu.VMEM((ROWS, 2 * DEPTH * SHARE), bf16),
             pltpu.SMEM((1, slots), jnp.int32),
@@ -360,13 +382,15 @@
             pltpu.VMEM((PIECES, 2, SIDE - 1, big, BLOCK), f32),
             pltpu.VMEM((PIECES, 2, big, BLOCK), f32),
             pltpu.VMEM((PIECES, 2, SIDE - 1, small, BLOCK), f32),
-            sems((4,)),
+            sems((5,)),
             sems,
-            sems((2 * REACH,)),
+            sems((2, 2 * REACH)),
             sems,
-            sems((2 * REACH - 1,)),
-        ]
-        + [sems] * 6
+            sems((2, 2 * REACH - 1)),
+            sems,
+            sems((2,)),
+        ]
+        + [sems] * 4
         + [sems((2,))]
         + [sems, sems((PIECES,))] * 4,
         compiler_params=pltpu.CompilerParams(

time: 53 us -> 52.3 us (0.987)
  Pallas kernels: 51.6 us -> 50.8 us
    pallas_call x1, Pallas kernels: 49.6 us -> 48.9 us  [on_device(): pl.pallas_call(gram_kernel, out_shape=[pltpu.VMEM((PANEL, PANEL), f32), p...]
where the time goes in v5:
time: 52.3 us; the launch traced here: 52.1 us
  Pallas kernels  50.8 us (97%)
  between operations  1.28 us (2%)
    pallas_call x1, Pallas kernels, on_device(): pl.pallas_call(gram_kernel, out_shape=[pltpu.VMEM((PANEL, PANEL), f32), p...  48.9 us
    pallas_call x1, Pallas kernels, on_device(): pl.pallas_call(solve_kernel, out_shape=[jax.ShapeDtypeStruct((PANEL, PANE...  1.97 us

profile of v5, /device:TPU:1, one launch (start us, length us, event | category | flops | bytes accessed | tf_op | source)
XLA Modules:
  0.0 52.1 jit_solution(14393208476364648669)
XLA Ops:
  1.3 48.9 %gram.1 = (f32[256,256]{1,0:T(8,128)S(1)}, f32[256,256]{1,0:T(8,128)S(1)}, f32[2,1024,128]{2,1,0:T(8,128)S(1)}) custom-call(bf16[16,256]{1,0:T(8,128)(2,1)} %panel_ref.1, bf16[7,16,2,16,128]{4,3,2,1,0:T(8,128)(2,1)} %bitcast.3, s32[1,7]{1,0:T(1,128)} %list_ref.1, s32[1,1]{1,0:T(1,128)S(6)} %copy.6.count_ref), custom_call_target="tpu_custom_call" | custom-call | tf_op jit(solution)/shard_map/gram/pallas_call | solution.py:365
  50.1 2.0 %solve.1 = (f32[256,256]{1,0:T(8,128)}, f32[1024,256]{1,0:T(8,128)}) custom-call(f32[256,256]{1,0:T(8,128)S(1)} %get-tuple-element.5.upper_ref, f32[256,256]{1,0:T(8,128)S(1)} %get-tuple-element.6.inverse_ref, f32[2,1024,128]{2,1,0:T(8,128)S(1)} %get-tuple-element.7.total_ref), custom_call_target="tpu_custom_call" | custom-call | tf_op jit(solution)/shard_map/solve/pallas_call | solution.py:401

commit v6 on v5

--- a/solution.py
+++ b/solution.py
@@ -25,9 +25,9 @@
 )
 FAR_FIRST_SIDE = (2, 1, 3)
 ORDER = (
-    ("sum", 0), ("sum", 1), ("half", 0), ("sum", 2), ("diag", 0), ("factor", 0), ("sum", 3), ("pass", 0), ("factor", 1),
-    ("pass", 1), ("factor", 2), ("pass", 2), ("factor", 3), ("pass", 3), ("factor", 4), ("factor", 5), ("factor", 6),
-    ("factor", 7),
+    ("share", 0), ("first", 0), ("first", 1), ("first", 2), ("first", 3), ("sum", 0), ("half", 0), ("sum", 1), ("sum", 2),
+    ("diag", 0), ("factor", 0), ("sum", 3), ("pass", 0), ("pass", 1), ("factor", 1), ("factor", 2), ("pass", 2), ("factor", 3),
+    ("pass", 3), ("factor", 4), ("factor", 5), ("factor", 6), ("factor", 7),
 )
 
 
@@ -285,29 +285,27 @@
     products(1, gathered1)
 
     others = diag_in.at[pl.ds(0, len(xy_ids))]
-    wait(others, ds_recv)
-    diag_sum = diag_in[0]
-    for k in range(1, SIDE * SIDE):
-        diag_sum = diag_sum + diag_in[k]
-    row = lax.broadcasted_iota(jnp.int32, (TILE, PANEL), 0) + (core * SIDE * SIDE + user) * TILE
-    col = lax.broadcasted_iota(jnp.int32, (TILE, PANEL), 1)
-    work[diag_rows(user), :] = diag_sum + jnp.where(row == col, 0.5, 0.0)
-    dg_copies = [
-        remote(work.at[diag_rows(user)], work.at[diag_rows(user)], dg_send, dg_recv, d)
-        for d in xy_ids
-    ]
-    start(dg_copies)
+    dg_copies = [remote(work.at[diag_rows(user)], work.at[diag_rows(user)], dg_send, dg_recv, d) for d in xy_ids]
     core_half = pl.ds(pl.multiple_of(core * BLOCK, BLOCK), BLOCK)
     half_copy = remote(work.at[core_half], work.at[core_half], half_sem.at[0], half_sem.at[1], core_id)
 
-    for q in range(PIECES):
-        wait(in1.at[q], s1_recv.at[q])
-        for h in range(2):
-            sum1[q, h] = part[half_of(q), big_rows(q, h, place[h]), :] + in1[q, h, 0] + in1[q, h, 1] + in1[q, h, 2]
-        start(s2[q])
-
     for what, n in ORDER:
-        if what == "half":
+        if what == "first":
+            wait(in1.at[n], s1_recv.at[n])
+            for h in range(2):
+                mine = part[half_of(n), big_rows(n, h, place[h]), :]
+                sum1[n, h] = mine + in1[n, h, 0] + in1[n, h, 1] + in1[n, h, 2]
+            start(s2[n])
+        elif what == "share":
+            wait(others, ds_recv)
+            diag_sum = diag_in[0]
+            for k in range(1, SIDE * SIDE):
+                diag_sum = diag_sum + diag_in[k]
+            row = lax.broadcasted_iota(jnp.int32, (TILE, PANEL), 0) + (core * SIDE * SIDE + user) * TILE
+            col = lax.broadcasted_iota(jnp.int32, (TILE, PANEL), 1)
+            work[diag_rows(user), :] = diag_sum + jnp.where(row == col, 0.5, 0.0)
+            start(dg_copies)
+        elif what == "half":
             wait(others, dg_recv)
             wait(others, dg_send)
             half_copy.start()

time: 52.3 us -> 52.1 us (level)
  no operation moved by 1% of the time
where the time goes in v6:
time: 52.1 us; the launch traced here: 52 us
  Pallas kernels  50.7 us (97%)
  between operations  1.28 us (2%)
    pallas_call x1, Pallas kernels, on_device(): pl.pallas_call(gram_kernel, out_shape=[pltpu.VMEM((PANEL, PANEL), f32), p...  48.7 us
    pallas_call x1, Pallas kernels, on_device(): pl.pallas_call(solve_kernel, out_shape=[jax.ShapeDtypeStruct((PANEL, PANE...  1.97 us

profile of v6, /device:TPU:1, one launch (start us, length us, event | category | flops | bytes accessed | tf_op | source)
XLA Modules:
  0.0 52.0 jit_solution(5502514340441002946)
XLA Ops:
  1.3 48.7 %gram.1 = (f32[256,256]{1,0:T(8,128)S(1)}, f32[256,256]{1,0:T(8,128)S(1)}, f32[2,1024,128]{2,1,0:T(8,128)S(1)}) custom-call(bf16[16,256]{1,0:T(8,128)(2,1)} %panel_ref.1, bf16[7,16,2,16,128]{4,3,2,1,0:T(8,128)(2,1)} %bitcast.3, s32[1,7]{1,0:T(1,128)} %list_ref.1, s32[1,1]{1,0:T(1,128)S(6)} %copy.6.count_ref), custom_call_target="tpu_custom_call" | custom-call | tf_op jit(solution)/shard_map/gram/pallas_call | solution.py:363
  50.0 2.0 %solve.1 = (f32[256,256]{1,0:T(8,128)}, f32[1024,256]{1,0:T(8,128)}) custom-call(f32[256,256]{1,0:T(8,128)S(1)} %get-tuple-element.5.upper_ref, f32[256,256]{1,0:T(8,128)S(1)} %get-tuple-element.6.inverse_ref, f32[2,1024,128]{2,1,0:T(8,128)S(1)} %get-tuple-element.7.total_ref), custom_call_target="tpu_custom_call" | custom-call | tf_op jit(solution)/shard_map/solve/pallas_call | solution.py:399
